TPU v7x, 128 devices: a whole 4x4x4 slice. The times are simulated.
128 devices in a mesh: row: 8 (over x, core), col: 16 (over z, y).
Axes of the slice: x: 4, y: 4, z: 4, core: 2. Of those that a mesh axis runs over, the one named last changes fastest.
Arguments:
- density: bfloat16 [6144, 6144], P('row', 'col'), may hold values from -5 to 5
- strips: bfloat16 [16384, 8, 128], P(('row', 'col')), may hold values from -5 to 5
- dest_device: int32 [16384, 1], P(('row', 'col')), may hold values from 0 to 127; in each aligned block of 128 rows (0 to 127, 128 to 255, ...) at most 2 rows name the same one
- atom_slot: int32 [16384], P(('row', 'col')), may hold values from 0 to 95
- block_slot: int32 [16384], P(('row', 'col')), may hold values from 0 to 2
- patterns: int32 [3, 48, 48], replicated, may hold values 0 or 1
Outputs:
- density_next: float32 [6144, 6144], P('row', 'col')
- response_next: float32 [6144, 6144], P('row', 'col')
Inputs may be any that keep to these rules, and one draw needn't show every extreme that they name: `dest_device`: of the 128 strips of one device, at most 2 name the same owner, and some owner is named that often.
All inputs are finite; a program needn't handle non-finite values.
Results may differ from a plain program's by a relative error of at most 0.0036.
Values may be sent and summed in bfloat16 or wider, within the bound.
A program may use at most 128 MiB of HBM per device.

v0:
```python
import math
import jax
import jax.numpy as jnp
from jax import lax
from jax.sharding import PartitionSpec as P

STEPS = 2
CAPACITY = 2


def tile_kept(patterns, which, row_offset, col_offset, block_rows, block_cols, block_width):
    window = lax.dynamic_slice(patterns[which], (row_offset, col_offset), (block_rows, block_cols))
    global_rows = row_offset + lax.iota(jnp.int32, block_rows)
    global_cols = col_offset + lax.iota(jnp.int32, block_cols)
    diagonal = (global_rows[:, None] == global_cols[None, :]).astype(jnp.int32)
    kept = jnp.maximum(window, diagonal).astype(jnp.float32)
    return jnp.repeat(jnp.repeat(kept, block_width, axis=0), block_width, axis=1)


def products(zeroth, linear):
    col_zero, col_first = (
        lax.all_gather(zeroth, "row", axis=0, tiled=True),
        lax.all_gather(linear, "row", axis=0, tiled=True),
    )
    pieces = (
        lax.all_gather(zeroth, "col", axis=1, tiled=True),
        lax.all_gather(linear, "col", axis=1, tiled=True),
    )
    square = jnp.dot(pieces[0], col_zero, preferred_element_type=jnp.float32)
    left_part = jnp.dot(pieces[0], col_first, preferred_element_type=jnp.float32)
    right_part = jnp.dot(pieces[1], col_zero, preferred_element_type=jnp.float32)
    return (square, left_part + right_part)


def on_device(density, strips, dest_device, atom_slot, block_slot, patterns):
    tile_rows, tile_cols = density.shape
    mesh_rows = lax.axis_size("row")
    mesh_cols = lax.axis_size("col")
    devices = mesh_rows * mesh_cols
    matrix_order = tile_rows * mesh_rows
    atom_width = strips.shape[1]
    block_width = strips.shape[2]
    block_rows = tile_rows // block_width
    block_cols = tile_cols // block_width
    row_offset = lax.axis_index("row") * block_rows
    col_offset = lax.axis_index("col") * block_cols
    kept_zero = tile_kept(patterns, 0, row_offset, col_offset, block_rows, block_cols, block_width)
    kept_first = tile_kept(patterns, 1, row_offset, col_offset, block_rows, block_cols, block_width)
    kept_field = tile_kept(patterns, 2, row_offset, col_offset, block_rows, block_cols, block_width)
    capacity = CAPACITY
    targets = dest_device[:, 0]
    matches = (targets[:, None] == lax.iota(jnp.int32, devices)[None, :]).astype(jnp.int32)
    before = jnp.cumsum(matches, axis=0) - matches
    ranking = jnp.sum(before * matches, axis=1)
    position = targets * capacity + ranking
    sent_strips = (
        jnp.zeros((devices * capacity, atom_width, block_width), strips.dtype)
        .at[position]
        .set(strips)
    )
    sent_atoms = jnp.full((devices * capacity,), -1, jnp.int32).at[position].set(atom_slot)
    sent_blocks = jnp.zeros((devices * capacity,), jnp.int32).at[position].set(block_slot)
    arrived = (
        lax.all_to_all(
            sent_strips.reshape(devices, capacity, atom_width, block_width),
            ("row", "col"),
            split_axis=0,
            concat_axis=0,
            tiled=True,
        ),
        lax.all_to_all(
            sent_atoms.reshape(devices, capacity),
            ("row", "col"),
            split_axis=0,
            concat_axis=0,
            tiled=True,
        ),
        lax.all_to_all(
            sent_blocks.reshape(devices, capacity),
            ("row", "col"),
            split_axis=0,
            concat_axis=0,
            tiled=True,
        ),
    )
    recv_strips = arrived[0].reshape(-1, atom_width * block_width)
    recv_atoms = arrived[1].reshape(-1)
    recv_blocks = arrived[2].reshape(-1)
    atoms_here = tile_rows // atom_width
    atom_match = recv_atoms[:, None] == lax.iota(jnp.int32, atoms_here)[None, :]
    block_match = recv_blocks[:, None] == lax.iota(jnp.int32, block_cols)[None, :]
    placing = (
        (atom_match[:, :, None] & block_match[:, None, :])
        .astype(jnp.bfloat16)
        .reshape(-1, atoms_here * block_cols)
    )
    summed = lax.dot_general(
        placing, recv_strips, (((0,), (0,)), ((), ())), preferred_element_type=jnp.float32
    )
    h_field = (
        summed.reshape(atoms_here, block_cols, atom_width, block_width)
        .transpose(0, 2, 1, 3)
        .reshape(tile_rows, tile_cols)
    )
    linear = (-(kept_field * h_field)).astype(jnp.bfloat16)
    zeroth = density
    inv_root = 1.0 / math.sqrt(matrix_order)
    new_zeroth = None
    new_linear = None
    for iteration in range(STEPS):
        square, crossed = products(zeroth, linear)
        if iteration % 2 == 0:
            new_zeroth = kept_zero * (square * inv_root)
            new_linear = kept_first * (crossed * inv_root)
        else:
            new_zeroth = kept_zero * (2.0 * zeroth.astype(jnp.float32) - square * inv_root)
            new_linear = kept_first * (2.0 * linear.astype(jnp.float32) - crossed * inv_root)
        zeroth = new_zeroth.astype(jnp.bfloat16)
        linear = new_linear.astype(jnp.bfloat16)
    return (new_zeroth, new_linear)


def solution(mesh):
    return jax.shard_map(
        on_device,
        mesh=mesh,
        in_specs=(
            P("row", "col"),
            P(("row", "col"), None, None),
            P(("row", "col"), None),
            P(("row", "col")),
            P(("row", "col")),
            P(),
        ),
        out_specs=(P("row", "col"), P("row", "col")),
        check_vma=False,
    )
```

profile of v0, /device:TPU:0, one launch (start us, length us, event | category | flops | bytes accessed | tf_op | source)
XLA Modules:
  0.0 541.6 jit_solution(12071236785653305353)
XLA Ops:
  10.3 1.1 scatter_custom_fusion.1
  12.2 11.1 %all-to-all-start.1 = ((s32[128,1,2]{2,1,0:T(1,128)}), s32[128,1,2]{2,1,0:T(1,128)S(1)}, u32[]{:S(2)}, u32[]{:S(2)}) async-start(s32[128,1,2]{2,1,0:T(1,128)} %bitcast.10), calls=%async_computation.1 | async-start | bytes 131072 | tf_op jit(solution)/shard_map/all_to_all | solution.py:78
  24.7 1.1 scatter_custom_fusion
  26.6 6.2 %all-to-all-done.1 = s32[128,1,2]{2,1,0:T(1,128)S(1)} async-done(((s32[128,1,2]{2,1,0:T(1,128)}), s32[128,1,2]{2,1,0:T(1,128)S(1)}, u32[]{:S(2)}, u32[]{:S(2)}) %all-to-all-start.1) | async-done | bytes 1056 | tf_op jit(solution)/shard_map/all_to_all | solution.py:78
  32.8 4.6 all-to-all-start
  37.5 0.9 broadcast_in_dim.49
  38.3 13.3 %scatter_fusion = bf16[256,8,128]{2,1,0:T(8,128)(2,1)} fusion(bf16[256,8,128]{2,1,0:T(8,128)(2,1)} %broadcast_in_dim.49, s32[128]{0:T(128)S(1)} %fusion.18, bf16[128,8,128]{2,1,0:T(8,128)(2,1)S(1)} %copy-done.2), kind=kCustom, calls=%fused_computation.2 | custom fusion | bytes 786944 | tf_op jit(solution)/shard_map/scatter | solution.py:59
  52.2 0.8 reduce.6
  53.2 9.8 %all-to-all-start.2 = ((bf16[128,2,8,128]{3,2,1,0:T(8,128)(2,1)}), bf16[128,2,8,128]{3,2,1,0:T(8,128)(2,1)S(1)}, u32[]{:S(2)}, u32[]{:S(2)}) async-start(bf16[128,2,8,128]{3,2,1,0:T(8,128)(2,1)} %bitcast.13), calls=%async_computation.2 | async-start | bytes 1048576 | tf_op jit(solution)/shard_map/all_to_all | solution.py:64
  64.5 12.2 %all-to-all-done.2 = bf16[128,2,8,128]{3,2,1,0:T(8,128)(2,1)S(1)} async-done(((bf16[128,2,8,128]{3,2,1,0:T(8,128)(2,1)}), bf16[128,2,8,128]{3,2,1,0:T(8,128)(2,1)S(1)}, u32[]{:S(2)}, u32[]{:S(2)}) %all-to-all-start.2) | async-done | bytes 524320 | tf_op jit(solution)/shard_map/all_to_all | solution.py:64
  78.4 0.9 fusion.12
  81.2 69.7 %all-gather.19.cloned.1.call-done = bf16[768,6144]{0,1:T(8,128)(2,1)} async-done(((bf16[768,384]{0,1:T(8,128)(2,1)}), bf16[768,6144]{0,1:T(8,128)(2,1)}) %all-gather.19.cloned.1.call-update) | async-done | bytes 9437200 | tf_op jit(solution)/shard_map/all_gather | solution.py:27
  150.9 9.0 %fusion.24 = f32[768,384]{1,0:T(8,128)S(1)} fusion(bf16[768,6144]{0,1:T(8,128)(2,1)} %all-gather.19.cloned.1.call-done, bf16[6144,384]{1,0:T(8,128)(2,1)} %all-gather.11.cloned.1.call-done), kind=kOutput, calls=%fused_computation.56 | convolution fusion | flops 3623878656 | bytes 15335424 | tf_op jit(solution)/shard_map/dot_general | solution.py:31
  159.9 27.1 %all-gather.17.cloned.1.call-done = bf16[6144,384]{0,1:T(8,128)(2,1)} async-done(((bf16[768,384]{0,1:T(8,128)(2,1)}), bf16[6144,384]{0,1:T(8,128)(2,1)}) %all-gather.17.cloned.1.call-update) | async-done | bytes 4718608 | tf_op jit(solution)/shard_map/all_gather | solution.py:23
  187.1 85.9 %all-gather.9.cloned.1.call-done = bf16[768,6144]{1,0:T(8,128)(2,1)} async-done(((bf16[768,384]{1,0:T(8,128)(2,1)}), bf16[768,6144]{1,0:T(8,128)(2,1)}) %all-gather.9.cloned.1.call-update) | async-done | bytes 9437200 | tf_op jit(solution)/shard_map/all_gather | solution.py:26
  272.9 9.8 %fusion.9 = bf16[768,384]{1,0:T(8,128)(2,1)} fusion(f32[768,384]{1,0:T(8,128)S(1)} %copy.40, f32[768,384]{1,0:T(8,128)S(1)} %fusion.24, bf16[6144,384]{0,1:T(8,128)(2,1)} %all-gather.17.cloned.1.call-done, bf16[768,6144]{1,0:T(8,128)(2,1)} %all-gather.9.cloned.1.call-done), kind=kOutput, calls=%fused_computation.17 | convolution fusion | flops 3625058304 | bytes 17104896 | tf_op jit(solution)/shard_map/dot_general | solution.py:30
  283.5 9.7 %fusion.10 = bf16[768,384]{1,0:T(8,128)(2,1)} fusion(f32[768,384]{1,0:T(8,128)S(1)} %copy.29, bf16[768,6144]{1,0:T(8,128)(2,1)} %all-gather.9.cloned.1.call-done, bf16[6144,384]{1,0:T(8,128)(2,1)} %all-gather.11.cloned.1.call-done), kind=kOutput, calls=%fused_computation.18 | convolution fusion | flops 3624763392 | bytes 15925248 | tf_op jit(solution)/shard_map/dot_general | solution.py:29
  294.8 21.6 %all-gather.21.cloned.1.call-done = bf16[6144,384]{1,0:T(8,128)(2,1)} async-done(((bf16[768,384]{1,0:T(8,128)(2,1)}), bf16[6144,384]{1,0:T(8,128)(2,1)}) %all-gather.21.cloned.1.call-update) | async-done | bytes 4718608 | tf_op jit(solution)/shard_map/all_gather | solution.py:23
  316.4 86.4 %all-gather.13.cloned.1.call-done = bf16[768,6144]{1,0:T(8,128)(2,1)} async-done(((bf16[768,384]{1,0:T(8,128)(2,1)}), bf16[768,6144]{1,0:T(8,128)(2,1)}) %all-gather.13.cloned.1.call-update) | async-done | bytes 9437200 | tf_op jit(solution)/shard_map/all_gather | solution.py:26
  402.9 9.8 %fusion.25 = f32[768,384]{1,0:T(8,128)} fusion(bf16[768,6144]{1,0:T(8,128)(2,1)} %all-gather.13.cloned.1.call-done, bf16[6144,384]{1,0:T(8,128)(2,1)} %all-gather.21.cloned.1.call-done), kind=kOutput, calls=%fused_computation.57 | convolution fusion | flops 3623878656 | bytes 15335424 | tf_op jit(solution)/shard_map/dot_general | solution.py:30
  412.6 26.0 %all-gather.15.cloned.1.call-done = bf16[6144,384]{1,0:T(8,128)(2,1)} async-done(((bf16[768,384]{1,0:T(8,128)(2,1)}), bf16[6144,384]{1,0:T(8,128)(2,1)}) %all-gather.15.cloned.1.call-update) | async-done | bytes 4718608 | tf_op jit(solution)/shard_map/all_gather | solution.py:22
  438.7 9.8 %fusion.2 = f32[768,384]{1,0:T(8,128)} fusion(f32[768,384]{1,0:T(8,128)S(1)} %copy.29, bf16[768,6144]{1,0:T(8,128)(2,1)} %all-gather.13.cloned.1.call-done, bf16[6144,384]{1,0:T(8,128)(2,1)} %all-gather.15.cloned.1.call-done, bf16[768,384]{1,0:T(8,128)(2,1)S(1)} %copy-done.1), kind=kOutput, calls=%fused_computation.9 | convolution fusion | flops 3625353216 | bytes 17104896 | tf_op jit(solution)/shard_map/dot_general | solution.py:29
  448.5 76.2 %all-gather.23.cloned.1.call-done = bf16[768,6144]{1,0:T(8,128)(2,1)} async-done(((bf16[768,384]{1,0:T(8,128)(2,1)}), bf16[768,6144]{1,0:T(8,128)(2,1)}) %all-gather.23.cloned.1.call-update) | async-done | bytes 9437200 | tf_op jit(solution)/shard_map/all_gather | solution.py:27
  524.7 10.1 %fusion.8 = f32[768,384]{1,0:T(8,128)} fusion(f32[768,384]{1,0:T(8,128)S(1)} %copy.40, f32[768,384]{1,0:T(8,128)} %fusion.25, bf16[768,6144]{1,0:T(8,128)(2,1)} %all-gather.23.cloned.1.call-done, bf16[6144,384]{1,0:T(8,128)(2,1)} %all-gather.15.cloned.1.call-done, bf16[768,384]{1,0:T(8,128)(2,1)S(1)} %copy-done), kind=kOutput, calls=%fused_computation.16 | convolution fusion | flops 3625648128 | bytes 18284544 | tf_op jit(solution)/shard_map/dot_general | solution.py:31
  (63 shorter events, 14.0 us)
Async XLA Ops:
  7.2 31.2 %copy-start.2 = (bf16[128,8,128]{2,1,0:T(8,128)(2,1)S(1)}, bf16[128,8,128]{2,1,0:T(8,128)(2,1)}, u32[]{:S(2)}) copy-start(bf16[128,8,128]{2,1,0:T(8,128)(2,1)} %param.7) | copy-start | bytes 786436
  7.2 74.1 %all-gather.11.cloned.1.call-start = ((), (), s32[]{:S(2)}) async-start(), calls=%async_computation.4 | async-start | bytes 5308416 | tf_op jit(solution)/shard_map/all_gather | solution.py:22
  12.2 20.6 %all-to-all-start.1 = ((s32[128,1,2]{2,1,0:T(1,128)}), s32[128,1,2]{2,1,0:T(1,128)S(1)}, u32[]{:S(2)}, u32[]{:S(2)}) async-start(s32[128,1,2]{2,1,0:T(1,128)} %bitcast.10), calls=%async_computation.1 | async-start | bytes 131072 | tf_op jit(solution)/shard_map/all_to_all | solution.py:78
  32.8 20.5 %all-to-all-start = ((s32[128,1,2]{2,1,0:T(1,128)}), s32[128,1,2]{2,1,0:T(1,128)S(1)}, u32[]{:S(2)}, u32[]{:S(2)}) async-start(s32[128,1,2]{2,1,0:T(1,128)} %bitcast.9), calls=%async_computation | async-start | bytes 131072 | tf_op jit(solution)/shard_map/all_to_all | solution.py:71
  53.2 23.4 %all-to-all-start.2 = ((bf16[128,2,8,128]{3,2,1,0:T(8,128)(2,1)}), bf16[128,2,8,128]{3,2,1,0:T(8,128)(2,1)S(1)}, u32[]{:S(2)}, u32[]{:S(2)}) async-start(bf16[128,2,8,128]{3,2,1,0:T(8,128)(2,1)} %bitcast.13), calls=%async_computation.2 | async-start | bytes 1048576 | tf_op jit(solution)/shard_map/all_to_all | solution.py:64
  63.0 87.9 %all-gather.19.cloned.1.call-start = ((), (), s32[]{:S(2)}) async-start(), calls=%async_computation.8 | async-start | bytes 10027008 | tf_op jit(solution)/shard_map/all_gather | solution.py:27
  79.3 107.8 %all-gather.17.cloned.1.call-start = ((), (), s32[]{:S(2)}) async-start(), calls=%async_computation.7 | async-start | bytes 5308416 | tf_op jit(solution)/shard_map/all_gather | solution.py:23
  80.0 192.9 %all-gather.9.cloned.1.call-start = ((), (), s32[]{:S(2)}) async-start(), calls=%async_computation.3 | async-start | bytes 10027008 | tf_op jit(solution)/shard_map/all_gather | solution.py:26
  80.6 235.8 %all-gather.21.cloned.1.call-start = ((), (), s32[]{:S(2)}) async-start(), calls=%async_computation.9 | async-start | bytes 5308416 | tf_op jit(solution)/shard_map/all_gather | solution.py:23
  282.8 120.1 %all-gather.13.cloned.1.call-start = ((), (), s32[]{:S(2)}) async-start(), calls=%async_computation.5 | async-start | bytes 10027008 | tf_op jit(solution)/shard_map/all_gather | solution.py:26
  293.3 145.4 %all-gather.15.cloned.1.call-start = ((), (), s32[]{:S(2)}) async-start(), calls=%async_computation.6 | async-start | bytes 5308416 | tf_op jit(solution)/shard_map/all_gather | solution.py:22
  294.0 230.6 %all-gather.23.cloned.1.call-start = ((), (), s32[]{:S(2)}) async-start(), calls=%async_computation.10 | async-start | bytes 10027008 | tf_op jit(solution)/shard_map/all_gather | solution.py:27
  294.8 143.9 %copy-start.1 = (bf16[768,384]{1,0:T(8,128)(2,1)S(1)}, bf16[768,384]{1,0:T(8,128)(2,1)}, u32[]{:S(2)}) copy-start(bf16[768,384]{1,0:T(8,128)(2,1)} %fusion.10) | copy-start | bytes 1769476
  412.6 112.0 %copy-start = (bf16[768,384]{1,0:T(8,128)(2,1)S(1)}, bf16[768,384]{1,0:T(8,128)(2,1)}, u32[]{:S(2)}) copy-start(bf16[768,384]{1,0:T(8,128)(2,1)} %fusion.9) | copy-start | bytes 1769476
Sparse Core Ops, SparseCore 0:
  9.7 38.0 all-gather.10
  79.4 71.4 all-gather.18
  153.2 33.8 all-gather.16
  189.0 83.8 all-gather.8
  282.9 33.4 all-gather.20
  319.0 83.8 all-gather.12
  405.1 33.4 all-gather.14
  440.8 83.8 all-gather.22
where the time goes:
time: 542 us
  waiting for transfers between devices  415 us (77%)
  matrix products  58.5 us (11%)
  starting transfers between devices  26 us (5%)
  local copies, waits for them, and re-layouts  22.7 us (4%)
  between operations  14.4 us (3%)
    all_gather x2, waiting for transfers between devices, products(): lax.all_gather(zeroth, 'col', axis=1, tiled=True)  172 us
    all_gather x2, waiting for transfers between devices, products(): lax.all_gather(linear, 'col', axis=1, tiled=True)  146 us
    all_gather x2, waiting for transfers between devices, products(): lax.all_gather(linear, 'row', axis=0, tiled=True)  48.8 us
    all_gather x2, waiting for transfers between devices, products(): lax.all_gather(zeroth, 'row', axis=0, tiled=True)  26 us
    dot_general x2, matrix products, products(): jnp.dot(pieces[0], col_first, preferred_element_type=jnp.float32)  19.6 us
    dot_general x2, matrix products, products(): square = jnp.dot(pieces[0], col_zero, preferred_element_type=jnp.float32)  19.5 us
    dot_general x2, matrix products, products(): jnp.dot(pieces[1], col_zero, preferred_element_type=jnp.float32)  19.1 us
    scatter x1, local copies, waits for them, and re-layouts, on_device(): sent_strips = jnp.zeros((devices * capacity, atom_width, block_width), st...  13.3 us
  transfers between devices with their start and end apart: 11, of which 9 were waited for; matrix products, arithmetic and copies ran while one was open for 12% of the time, Pallas kernels for 0%

commit v1 on v0

--- a/solution.py
+++ b/solution.py
@@ -6,6 +6,11 @@
 
 STEPS = 2
 CAPACITY = 2
+
+
+def gather_from_all(value, axis, dim):
+    copies = jnp.concatenate([value] * lax.axis_size(axis), axis=dim)
+    return lax.all_to_all(copies, axis, dim, dim, tiled=True)
 
 
 def tile_kept(patterns, which, row_offset, col_offset, block_rows, block_cols, block_width):
@@ -19,7 +24,7 @@
 
 def products(zeroth, linear):
     col_zero, col_first = (
-        lax.all_gather(zeroth, "row", axis=0, tiled=True),
+        gather_from_all(zeroth, "row", 0),
         lax.all_gather(linear, "row", axis=0, tiled=True),
     )
     pieces = (

time: 542 us -> 425 us (0.78)
  waiting for transfers between devices: 415 us -> 214 us
  blocking collectives: 0 us -> 59.3 us
  local copies, waits for them, and re-layouts: 22.7 us -> 43.9 us
    all_gather x2, waiting for transfers between devices: 172 us -> 0.01 us  [products(): lax.all_gather(zeroth, 'col', axis=1, tiled=True)]
    all_gather x2, waiting for transfers between devices: 146 us -> 85 us  [products(): lax.all_gather(linear, 'col', axis=1, tiled=True)]
    all_to_all x0 -> x1, blocking collectives: none -> 59.3 us  [gather_from_all(): return lax.all_to_all(copies, axis, dim, dim, tiled=True)]
    all_to_all x0 -> x1, waiting for transfers between devices: none -> 55 us  [gather_from_all(): return lax.all_to_all(copies, axis, dim, dim, tiled=True)]
    all_gather x2 -> x0, waiting for transfers between devices: 26 us -> none  [products(): lax.all_gather(zeroth, 'row', axis=0, tiled=True)]
    unnamed x13 -> x30, local copies, waits for them, and re-layouts: 0.34 us -> 11.4 us
    all_to_all x0 -> x2, local copies, waits for them, and re-layouts: none -> 9.29 us  [gather_from_all(): return lax.all_to_all(copies, axis, dim, dim, tiled=True)]
  transfers between devices with their start and end apart: 11 -> 10, of which waited for: 9 -> 7; matrix products, arithmetic and copies ran while one was open for 12% -> 21% of each run, Pallas kernels for 0% -> 0%
where the time goes in v1:
time: 425 us; the launch traced here: 423 us
  waiting for transfers between devices  214 us (50%)
  blocking collectives  59.3 us (14%)
  matrix products  55.1 us (13%)
  local copies, waits for them, and re-layouts  43.9 us (10%)
  starting transfers between devices  30.5 us (7%)
  between operations  14.4 us (3%)
  other arithmetic  5.14 us (1%)
    all_gather x2, waiting for transfers between devices, products(): lax.all_gather(linear, 'col', axis=1, tiled=True)  85 us
    all_to_all x1, blocking collectives, gather_from_all(): return lax.all_to_all(copies, axis, dim, dim, tiled=True)  59.3 us
    all_to_all x1, waiting for transfers between devices, gather_from_all(): return lax.all_to_all(copies, axis, dim, dim, tiled=True)  55 us
    all_gather x2, waiting for transfers between devices, products(): lax.all_gather(linear, 'row', axis=0, tiled=True)  54.1 us
    dot_general x2, matrix products, products(): square = jnp.dot(pieces[0], col_zero, preferred_element_type=jnp.float32)  19 us
    dot_general x2, matrix products, products(): jnp.dot(pieces[0], col_first, preferred_element_type=jnp.float32)  18.3 us
    dot_general x2, matrix products, products(): jnp.dot(pieces[1], col_zero, preferred_element_type=jnp.float32)  17.5 us
    scatter x1, local copies, waits for them, and re-layouts, on_device(): sent_strips = jnp.zeros((devices * capacity, atom_width, block_width), st...  14 us
  transfers between devices with their start and end apart: 10, of which 7 were waited for; matrix products, arithmetic and copies ran while one was open for 21% of the time, Pallas kernels for 0%

profile of v1, /device:TPU:0, one launch (start us, length us, event | category | flops | bytes accessed | tf_op | source)
XLA Modules:
  0.0 422.8 jit_solution(11591837071736019821)
XLA Ops:
  12.2 11.1 %all-to-all-start.3 = ((s32[128,1,2]{2,1,0:T(1,128)}), s32[128,1,2]{2,1,0:T(1,128)S(1)}, u32[]{:S(2)}, u32[]{:S(2)}) async-start(s32[128,1,2]{2,1,0:T(1,128)} %bitcast.14), calls=%async_computation.3 | async-start | bytes 131072 | tf_op jit(solution)/shard_map/all_to_all | solution.py:83
  26.5 6.2 %all-to-all-done.3 = s32[128,1,2]{2,1,0:T(1,128)S(1)} async-done(((s32[128,1,2]{2,1,0:T(1,128)}), s32[128,1,2]{2,1,0:T(1,128)S(1)}, u32[]{:S(2)}, u32[]{:S(2)}) %all-to-all-start.3) | async-done | bytes 1056 | tf_op jit(solution)/shard_map/all_to_all | solution.py:83
  32.8 4.6 %all-to-all-start.2 = ((s32[128,1,2]{2,1,0:T(1,128)}), s32[128,1,2]{2,1,0:T(1,128)S(1)}, u32[]{:S(2)}, u32[]{:S(2)}) async-start(s32[128,1,2]{2,1,0:T(1,128)} %bitcast.13), calls=%async_computation.2 | async-start | bytes 131072 | tf_op jit(solution)/shard_map/all_to_all | solution.py:76
  38.3 14.0 %scatter_fusion = bf16[256,8,128]{2,1,0:T(8,128)(2,1)} fusion(bf16[256,8,128]{2,1,0:T(8,128)(2,1)} %broadcast_in_dim.49, s32[128]{0:T(128)S(1)} %fusion.15, bf16[128,8,128]{2,1,0:T(8,128)(2,1)} %param.7), kind=kCustom, calls=%fused_computation.2 | custom fusion | bytes 786944 | tf_op jit(solution)/shard_map/scatter | solution.py:64
  53.8 9.7 %all-to-all-start.4 = ((bf16[128,2,8,128]{3,2,1,0:T(8,128)(2,1)}), bf16[128,2,8,128]{3,2,1,0:T(8,128)(2,1)S(1)}, u32[]{:S(2)}, u32[]{:S(2)}) async-start(bf16[128,2,8,128]{3,2,1,0:T(8,128)(2,1)} %bitcast.17), calls=%async_computation.4 | async-start | bytes 1048576 | tf_op jit(solution)/shard_map/all_to_all | solution.py:69
  64.9 12.2 %all-to-all-done.4 = bf16[128,2,8,128]{3,2,1,0:T(8,128)(2,1)S(1)} async-done(((bf16[128,2,8,128]{3,2,1,0:T(8,128)(2,1)}), bf16[128,2,8,128]{3,2,1,0:T(8,128)(2,1)S(1)}, u32[]{:S(2)}, u32[]{:S(2)}) %all-to-all-start.4) | async-done | bytes 524320 | tf_op jit(solution)/shard_map/all_to_all | solution.py:69
  81.4 2.2 copy-done.3
  83.6 4.6 %all-to-all-start = ((bf16[8,768,384]{2,1,0:T(8,128)(2,1)}), bf16[8,768,384]{2,1,0:T(8,128)(2,1)}, u32[]{:S(2)}, u32[]{:S(2)}) async-start(bf16[8,768,384]{2,1,0:T(8,128)(2,1)} %bitcast.113), calls=%async_computation | async-start | bytes 9437184 | tf_op jit(solution)/shard_map/all_to_all | solution.py:13
  88.5 55.0 %all-to-all-done = bf16[8,768,384]{2,1,0:T(8,128)(2,1)} async-done(((bf16[8,768,384]{2,1,0:T(8,128)(2,1)}), bf16[8,768,384]{2,1,0:T(8,128)(2,1)}, u32[]{:S(2)}, u32[]{:S(2)}) %all-to-all-start) | async-done | bytes 4718624 | tf_op jit(solution)/shard_map/all_to_all | solution.py:13
  143.5 10.3 %constant_dynamic-update-slice_fusion.15 = (bf16[6144,384]{0,1:T(8,128)(2,1)}, bf16[768,384]{0,1:T(8,128)(2,1)}) fusion(bf16[6144,384]{1,0:T(8,128)(2,1)} %bitcast.3, bf16[768,6144]{1,0:T(8,128)(2,1)} %all-gather.7.cloned.1.call-done, f32[768,3]{0,1:T(4,128)S(1)} %bitcast.120), kind=kOutput, calls=%fused_computation.47 | convolution fusion | flops 3624763392 | bytes 15344640 | tf_op jit(solution)/shard_map/dot_general | solution.py:34
  153.9 25.1 %all-gather.13.cloned.1.call-done = bf16[768,6144]{0,1:T(8,128)(2,1)} async-done(((bf16[768,384]{0,1:T(8,128)(2,1)}), bf16[768,6144]{0,1:T(8,128)(2,1)}) %all-gather.13.cloned.1.call-update) | async-done | bytes 9437200 | tf_op jit(solution)/shard_map/all_gather | solution.py:32
  179.0 8.7 %fusion.21 = f32[768,384]{0,1:T(8,128)S(1)} fusion(bf16[768,6144]{0,1:T(8,128)(2,1)} %all-gather.13.cloned.1.call-done, bf16[6144,384]{1,0:T(8,128)(2,1)} %bitcast.3), kind=kOutput, calls=%fused_computation.74 | convolution fusion | flops 3623878656 | bytes 15335424 | tf_op jit(solution)/shard_map/dot_general | solution.py:36
  187.7 27.4 %all-gather.11.cloned.1.call-done = bf16[6144,384]{0,1:T(8,128)(2,1)} async-done(((bf16[768,384]{0,1:T(8,128)(2,1)}), bf16[6144,384]{0,1:T(8,128)(2,1)}) %all-gather.11.cloned.1.call-update) | async-done | bytes 4718608 | tf_op jit(solution)/shard_map/all_gather | solution.py:28
  215.1 9.8 %fusion.6 = bf16[768,384]{0,1:T(8,128)(2,1)} fusion(f32[768,384]{0,1:T(8,128)S(1)} %fusion.21, bf16[6144,384]{0,1:T(8,128)(2,1)} %all-gather.11.cloned.1.call-done, bf16[768,6144]{1,0:T(8,128)(2,1)} %all-gather.7.cloned.1.call-done, f32[768,3]{0,1:T(4,128)S(1)} %bitcast.122), kind=kOutput, calls=%fused_computation.19 | convolution fusion | flops 3625058304 | bytes 15934464 | tf_op jit(solution)/shard_map/dot_general | solution.py:35
  232.1 2.6 copy.84
  234.7 59.3 %all_to_all.47 = bf16[8,768,384]{1,2,0:T(8,128)(2,1)} all-to-all(bf16[8,768,384]{1,2,0:T(8,128)(2,1)S(1)} %bitcast.109), channel_id=1, replica_groups=mesh['row'=8,'col'=16] {'row'}, dimensions={0} | all-to-all | bytes 9437184 | tf_op jit(solution)/shard_map/all_to_all | solution.py:13
  294.0 6.6 %copy.49 = bf16[8,768,384]{2,1,0:T(8,128)(2,1)} copy(bf16[8,768,384]{1,2,0:T(8,128)(2,1)} %all_to_all.47) | data formatting | bytes 9437184 | tf_op jit(solution)/shard_map/all_to_all | solution.py:13
  300.7 8.8 %bitcast_multiply_fusion.2 = f32[768,384]{0,1:T(8,128)S(1)} fusion(bf16[768,6144]{0,1:T(8,128)(2,1)} %all-gather.9.cloned.1.call-done, bf16[6144,384]{1,0:T(8,128)(2,1)} %bitcast.110, bf16[768,384]{0,1:T(8,128)(2,1)S(1)} %copy-done, f32[768,3]{0,1:T(4,128)S(1)} %bitcast.121), kind=kOutput, calls=%fused_computation.6 | convolution fusion | flops 3625353216 | bytes 15934464 | tf_op jit(solution)/shard_map/dot_general | solution.py:34
  309.4 1.4 copy.62
  310.8 59.9 %all-gather.17.cloned.1.call-done = bf16[768,6144]{0,1:T(8,128)(2,1)} async-done(((bf16[768,384]{0,1:T(8,128)(2,1)}), bf16[768,6144]{0,1:T(8,128)(2,1)}) %all-gather.17.cloned.1.call-update) | async-done | bytes 9437200 | tf_op jit(solution)/shard_map/all_gather | solution.py:32
  370.7 8.8 %fusion.22 = f32[768,384]{0,1:T(8,128)S(1)} fusion(bf16[768,6144]{0,1:T(8,128)(2,1)} %all-gather.17.cloned.1.call-done, bf16[6144,384]{1,0:T(8,128)(2,1)} %bitcast.111), kind=kOutput, calls=%fused_computation.75 | convolution fusion | flops 3623878656 | bytes 15335424 | tf_op jit(solution)/shard_map/dot_general | solution.py:36
  379.5 26.7 %all-gather.15.cloned.1.call-done = bf16[6144,384]{0,1:T(8,128)(2,1)} async-done(((bf16[768,384]{0,1:T(8,128)(2,1)}), bf16[6144,384]{0,1:T(8,128)(2,1)}) %all-gather.15.cloned.1.call-update) | async-done | bytes 4718608 | tf_op jit(solution)/shard_map/all_gather | solution.py:28
  406.2 8.4 %bitcast_multiply_fusion = f32[768,384]{0,1:T(8,128)S(1)} fusion(f32[768,384]{0,1:T(8,128)S(1)} %fusion.22, bf16[6144,384]{0,1:T(8,128)(2,1)} %all-gather.15.cloned.1.call-done, bf16[768,6144]{0,1:T(8,128)(2,1)} %all-gather.9.cloned.1.call-done, bf16[768,384]{0,1:T(8,128)(2,1)S(1)} %copy-done.2, f32[768,3]{0,1:T(4,128)S(1)} %bitcast.123), kind=kOutput, calls=%fused_computation.4 | convolution fusion | flops 3625648128 | bytes 17114112 | tf_op jit(solution)/shard_map/dot_general | solution.py:35
  414.6 1.4 copy.63
  (77 shorter events, 23.5 us)
Async XLA Ops:
  7.2 136.3 %all-gather.7.cloned.1.call-start = ((), (), s32[]{:S(2)}) async-start(), calls=%async_computation.5 | async-start | bytes 10027008 | tf_op jit(solution)/shard_map/all_gather | solution.py:31
  12.2 20.6 %all-to-all-start.3 = ((s32[128,1,2]{2,1,0:T(1,128)}), s32[128,1,2]{2,1,0:T(1,128)S(1)}, u32[]{:S(2)}, u32[]{:S(2)}) async-start(s32[128,1,2]{2,1,0:T(1,128)} %bitcast.14), calls=%async_computation.3 | async-start | bytes 131072 | tf_op jit(solution)/shard_map/all_to_all | solution.py:83
  32.8 21.0 %all-to-all-start.2 = ((s32[128,1,2]{2,1,0:T(1,128)}), s32[128,1,2]{2,1,0:T(1,128)S(1)}, u32[]{:S(2)}, u32[]{:S(2)}) async-start(s32[128,1,2]{2,1,0:T(1,128)} %bitcast.13), calls=%async_computation.2 | async-start | bytes 131072 | tf_op jit(solution)/shard_map/all_to_all | solution.py:76
  53.8 23.4 %all-to-all-start.4 = ((bf16[128,2,8,128]{3,2,1,0:T(8,128)(2,1)}), bf16[128,2,8,128]{3,2,1,0:T(8,128)(2,1)S(1)}, u32[]{:S(2)}, u32[]{:S(2)}) async-start(bf16[128,2,8,128]{3,2,1,0:T(8,128)(2,1)} %bitcast.17), calls=%async_computation.4 | async-start | bytes 1048576 | tf_op jit(solution)/shard_map/all_to_all | solution.py:69
  63.5 115.5 %all-gather.13.cloned.1.call-start = ((), (), s32[]{:S(2)}) async-start(), calls=%async_computation.8 | async-start | bytes 10027008 | tf_op jit(solution)/shard_map/all_gather | solution.py:32
  77.4 3.1 copy-start.1
  79.8 135.3 %all-gather.11.cloned.1.call-start = ((), (), s32[]{:S(2)}) async-start(), calls=%async_computation.7 | async-start | bytes 5308416 | tf_op jit(solution)/shard_map/all_gather | solution.py:28
  81.4 2.2 copy-start.3
  83.6 59.9 %all-to-all-start = ((bf16[8,768,384]{2,1,0:T(8,128)(2,1)}), bf16[8,768,384]{2,1,0:T(8,128)(2,1)}, u32[]{:S(2)}, u32[]{:S(2)}) async-start(bf16[8,768,384]{2,1,0:T(8,128)(2,1)} %bitcast.113), calls=%async_computation | async-start | bytes 9437184 | tf_op jit(solution)/shard_map/all_to_all | solution.py:13
  88.2 212.5 %all-gather.9.cloned.1.call-start = ((), (), s32[]{:S(2)}) async-start(), calls=%async_computation.6 | async-start | bytes 10027008 | tf_op jit(solution)/shard_map/all_gather | solution.py:31
  153.8 217.0 %all-gather.17.cloned.1.call-start = ((), (), s32[]{:S(2)}) async-start(), calls=%async_computation.10 | async-start | bytes 10027008 | tf_op jit(solution)/shard_map/all_gather | solution.py:32
  215.1 10.4 %copy-start = (bf16[768,384]{0,1:T(8,128)(2,1)S(1)}, bf16[768,384]{0,1:T(8,128)(2,1)}, u32[]{:S(2)}) copy-start(bf16[768,384]{0,1:T(8,128)(2,1)} %get-tuple-element.17) | copy-start | bytes 1769476
  225.0 181.2 %all-gather.15.cloned.1.call-start = ((), (), s32[]{:S(2)}) async-start(), calls=%async_computation.9 | async-start | bytes 5308416 | tf_op jit(solution)/shard_map/all_gather | solution.py:28
  310.8 95.3 %copy-start.2 = (bf16[768,384]{0,1:T(8,128)(2,1)S(1)}, bf16[768,384]{0,1:T(8,128)(2,1)}, u32[]{:S(2)}) copy-start(bf16[768,384]{0,1:T(8,128)(2,1)} %fusion.6) | copy-start | bytes 1769476
Sparse Core Ops, SparseCore 0:
  10.1 92.5 all-gather.6
  105.4 73.5 all-gather.12
  181.3 33.8 all-gather.10
  217.7 75.6 all-gather.8
  295.4 75.2 all-gather.16
  372.3 33.8 all-gather.14
